TPU v7x, 32 devices: a whole 2x2x4 slice. The times are simulated.
32 devices in a mesh: dp: 8 (over z, x), tensor: 4 (over y, core).
Axes of the slice: x: 2, y: 2, z: 4, core: 2. Of those that a mesh axis runs over, the one named last changes fastest.
Arguments:
- tokens: bfloat16 [24576, 768], P('dp'), may hold values from -6 to 6
- cotangent: bfloat16 [24576, 768], P('dp'), may hold values from -6 to 6
- documents: int32 [24, 1024], P('dp'), may hold values from 0 to 7, never falling along the last dimension, each value on 1 to 512 neighbouring positions
- w_qkv: float32 [768, 3, 768], P('dp', None, 'tensor'), may hold values from -0.21875 to 0.21875
- w_out: float32 [768, 768], P('tensor', 'dp'), may hold values from -0.625 to 0.625
- w_fc: float32 [768, 3072], P('dp', 'tensor'), may hold values from -0.21875 to 0.21875
- w_proj: float32 [3072, 768], P('tensor', 'dp'), may hold values from -0.109375 to 0.109375
- vectors: float32 [12, 768], P(None, 'dp'), may hold values from -4 to 4, as said below
- first_qkv: float32 [768, 3, 768], P('dp', None, 'tensor'), may hold values from -0.00025017266 to 0.00025017266
- first_out: float32 [768, 768], P('tensor', 'dp'), may hold values from -0.00025017266 to 0.00025017266
- first_fc: float32 [768, 3072], P('dp', 'tensor'), may hold values from -0.00025017266 to 0.00025017266
- first_proj: float32 [3072, 768], P('tensor', 'dp'), may hold values from -0.00025017266 to 0.00025017266
- first_vec: float32 [12, 768], P(None, 'dp'), may hold values from -0.00090152305 to 0.00090152305
- second_qkv: float32 [768, 3, 768], P('dp', None, 'tensor'), may hold values from 7.0550676e-11 to 1.1288108e-09
- second_out: float32 [768, 768], P('tensor', 'dp'), may hold values from 7.0550676e-11 to 1.1288108e-09
- second_fc: float32 [768, 3072], P('dp', 'tensor'), may hold values from 7.0550676e-11 to 1.1288108e-09
- second_proj: float32 [3072, 768], P('tensor', 'dp'), may hold values from 7.0550676e-11 to 1.1288108e-09
- second_vec: float32 [12, 768], P(None, 'dp'), may hold values from 1.1288108e-09 to 1.8060973e-08
Outputs:
- output: bfloat16 [24576, 768], P('dp')
- input_grad: bfloat16 [24576, 768], P('dp')
- grad_norm: float32 [], replicated
- new_qkv: float32 [768, 3, 768], P('dp', None, 'tensor')
- new_out: float32 [768, 768], P('tensor', 'dp')
- new_fc: float32 [768, 3072], P('dp', 'tensor')
- new_proj: float32 [3072, 768], P('tensor', 'dp')
- new_vectors: float32 [12, 768], P(None, 'dp')
- mean_qkv: float32 [768, 3, 768], P('dp', None, 'tensor')
- mean_out: float32 [768, 768], P('tensor', 'dp')
- mean_fc: float32 [768, 3072], P('dp', 'tensor')
- mean_proj: float32 [3072, 768], P('tensor', 'dp')
- mean_vectors: float32 [12, 768], P(None, 'dp')
- square_qkv: float32 [768, 3, 768], P('dp', None, 'tensor')
- square_out: float32 [768, 768], P('tensor', 'dp')
- square_fc: float32 [768, 3072], P('dp', 'tensor')
- square_proj: float32 [3072, 768], P('tensor', 'dp')
- square_vectors: float32 [12, 768], P(None, 'dp')
Inputs may be any that keep to these rules, and one draw needn't show every extreme that they name: `documents`: document numbers never fall along a row; each document has 1 to 512 tokens, and some document of each row has exactly 512. `vectors`: gains near one and biases of order one.
All inputs are finite; a program needn't handle non-finite values.
Results may differ from a plain program's by a relative error of at most 0.02.
Values may be sent and summed in bfloat16 or wider, within the bound.
A program may use at most 192 MiB of HBM per device.

v0:
```python
import math

import jax
import jax.numpy as jnp
from jax import lax
from jax.sharding import PartitionSpec as P

D = 768
HD = 64
FF = 3072
STEP = 10


beta_one = 0.9
beta_two = 0.999
rate_qkv = 0.03
rate_out = 0.08
rate_fc = 0.03
rate_proj = 0.02
rate_vec = 0.6
decay_rate = 0.01
epsilon = 1e-08
max_norm = 1.0


def normalize(hidden, gain_row, bias_row):
    average = jnp.mean(hidden, -1, keepdims=True)
    centred = hidden - average
    inverse = lax.rsqrt(jnp.mean(centred * centred, -1, keepdims=True) + 1e-05)
    normed_unit = centred * inverse
    return (normed_unit * gain_row + bias_row, normed_unit, inverse)


def normalize_back(grad_rows, normed_unit, inverse, gain_row):
    scaled = grad_rows * gain_row
    return inverse * (
        scaled
        - jnp.mean(scaled, -1, keepdims=True)
        - normed_unit * jnp.mean(scaled * normed_unit, -1, keepdims=True)
    )


def gelu_tanh(values):
    return jax.nn.gelu(values, approximate=True)


def masked_scores(queries, key_rows, doc_ids):
    raw_scores = jnp.einsum("qhe,khe->hqk", queries, key_rows, preferred_element_type=jnp.float32)
    places = jnp.arange(doc_ids.shape[0])
    allowed = (doc_ids[:, None] == doc_ids[None, :]) & (places[:, None] >= places[None, :])
    return jnp.where(allowed[None], raw_scores * (1.0 / math.sqrt(HD)), -1e30)


def attend_forward(pieces):
    queries, key_rows, value_rows, doc_ids = pieces
    scores = masked_scores(queries, key_rows, doc_ids)
    highest = jnp.max(scores, -1, keepdims=True)
    exponent = jnp.exp(scores - highest)
    totals = jnp.sum(exponent, -1, keepdims=True)
    attention_weights = (exponent / totals).astype(jnp.bfloat16)
    context = jnp.einsum(
        "hqk,khe->qhe", attention_weights, value_rows, preferred_element_type=jnp.float32
    )
    return (context, (highest + jnp.log(totals))[..., 0])


def attend_backward(pieces):
    queries, key_rows, value_rows, grad_context, doc_ids, log_sums = pieces
    scores = masked_scores(queries, key_rows, doc_ids)
    exact_weights = jnp.exp(scores - log_sums[..., None])
    grad_weights = jnp.einsum(
        "qhe,khe->hqk", grad_context, value_rows, preferred_element_type=jnp.float32
    )
    centre = jnp.sum(exact_weights * grad_weights, -1, keepdims=True)
    grad_scores = (exact_weights * (grad_weights - centre)).astype(jnp.bfloat16)
    grad_values = jnp.einsum(
        "hqk,qhe->khe",
        exact_weights.astype(jnp.bfloat16),
        grad_context,
        preferred_element_type=jnp.float32,
    ).astype(jnp.bfloat16)
    grad_queries = (
        jnp.einsum("hqk,khe->qhe", grad_scores, key_rows, preferred_element_type=jnp.float32)
        * (1.0 / math.sqrt(HD))
    ).astype(jnp.bfloat16)
    grad_keys = (
        jnp.einsum("hqk,qhe->khe", grad_scores, queries, preferred_element_type=jnp.float32)
        * (1.0 / math.sqrt(HD))
    ).astype(jnp.bfloat16)
    return (grad_queries, grad_keys, grad_values)


def adam_step(weight, gradient, first, second, rate, decay):
    first = beta_one * first + (1.0 - beta_one) * gradient
    second = beta_two * second + (1.0 - beta_two) * gradient * gradient
    first_hat = first / (1.0 - beta_one**STEP)
    second_hat = second / (1.0 - beta_two**STEP)
    weight = weight - rate * (first_hat / (jnp.sqrt(second_hat) + epsilon) + decay * weight)
    return (weight, first, second)


def body(
    tokens,
    cotangent,
    documents,
    w_qkv,
    w_out,
    w_fc,
    w_proj,
    vectors,
    first_qkv,
    first_out,
    first_fc,
    first_proj,
    first_vec,
    second_qkv,
    second_out,
    second_fc,
    second_proj,
    second_vec,
):
    tensor_rank = lax.axis_index("tensor")
    head_only = jnp.where(tensor_rank == 0, 1.0, 0.0).astype(jnp.float32)
    full_qkv, full_out, full_fc, full_proj, full_vec = (
        lax.all_gather(w_qkv.astype(jnp.bfloat16), "dp", axis=0, tiled=True),
        lax.all_gather(w_out.astype(jnp.bfloat16), "dp", axis=1, tiled=True),
        lax.all_gather(w_fc.astype(jnp.bfloat16), "dp", axis=0, tiled=True),
        lax.all_gather(w_proj.astype(jnp.bfloat16), "dp", axis=1, tiled=True),
        lax.all_gather(vectors.astype(jnp.bfloat16), "dp", axis=1, tiled=True),
    )
    local_width = full_qkv.shape[2]
    hidden_width = full_fc.shape[1]
    row_count = tokens.shape[0]
    split_shape = (documents.shape[0], documents.shape[1], local_width // HD, HD)
    params = full_vec.astype(jnp.float32)
    query_bias = lax.dynamic_slice_in_dim(params[2], tensor_rank * local_width, local_width)
    value_bias = lax.dynamic_slice_in_dim(params[3], tensor_rank * local_width, local_width)
    fc_bias = lax.dynamic_slice_in_dim(
        params[8:].reshape(FF), tensor_rank * hidden_width, hidden_width
    )
    qkv_matrix = full_qkv.reshape(D, 3 * local_width)
    inputs = tokens.astype(jnp.float32)
    grad_output = cotangent.astype(jnp.float32)
    normed, unit_one, inverse_one = normalize(inputs, params[0], params[1])
    normed_low = normed.astype(jnp.bfloat16)
    joined_rows = jnp.dot(normed_low, qkv_matrix, preferred_element_type=jnp.float32)
    queries = (joined_rows[:, :local_width] + query_bias).astype(jnp.bfloat16).reshape(split_shape)
    key_rows = (
        joined_rows[:, local_width : 2 * local_width].astype(jnp.bfloat16).reshape(split_shape)
    )
    value_rows = (
        (joined_rows[:, 2 * local_width :] + value_bias).astype(jnp.bfloat16).reshape(split_shape)
    )
    context, log_sums = lax.map(attend_forward, (queries, key_rows, value_rows, documents))
    context_low = context.reshape(row_count, local_width).astype(jnp.bfloat16)
    attn_partial = jnp.dot(context_low, full_out, preferred_element_type=jnp.float32)
    middle = (
        inputs
        + lax.psum(attn_partial.astype(jnp.bfloat16), "tensor").astype(jnp.float32)
        + params[4]
    )
    normed_two, unit_two, inverse_two = normalize(middle, params[5], params[6])
    normed_two_low = normed_two.astype(jnp.bfloat16)
    pre_act = jnp.dot(normed_two_low, full_fc, preferred_element_type=jnp.float32) + fc_bias
    activated, gelu_pull = jax.vjp(gelu_tanh, pre_act)
    activated_low = activated.astype(jnp.bfloat16)
    mlp_partial = jnp.dot(activated_low, full_proj, preferred_element_type=jnp.float32)
    output = (
        middle
        + lax.psum(mlp_partial.astype(jnp.bfloat16), "tensor").astype(jnp.float32)
        + params[7]
    ).astype(jnp.bfloat16)
    grad_proj = jnp.dot(activated_low.T, cotangent, preferred_element_type=jnp.float32)
    grad_act = jnp.dot(cotangent, full_proj.T, preferred_element_type=jnp.float32).astype(
        jnp.bfloat16
    )
    grad_pre = gelu_pull(grad_act.astype(jnp.float32))[0].astype(jnp.bfloat16)
    grad_fc = jnp.dot(normed_two_low.T, grad_pre, preferred_element_type=jnp.float32)
    back_two_partial = jnp.dot(grad_pre, full_fc.T, preferred_element_type=jnp.float32)
    grad_normed_two = lax.psum(back_two_partial.astype(jnp.bfloat16), "tensor").astype(jnp.float32)
    grad_middle = grad_output + normalize_back(grad_normed_two, unit_two, inverse_two, params[5])
    grad_attn = grad_middle.astype(jnp.bfloat16)
    grad_wout = jnp.dot(context_low.T, grad_attn, preferred_element_type=jnp.float32)
    grad_context = jnp.dot(grad_attn, full_out.T, preferred_element_type=jnp.float32).astype(
        jnp.bfloat16
    )
    grad_q, grad_k, grad_v = lax.map(
        attend_backward,
        (queries, key_rows, value_rows, grad_context.reshape(split_shape), documents, log_sums),
    )
    grad_q = grad_q.reshape(row_count, local_width)
    grad_v = grad_v.reshape(row_count, local_width)
    grad_joined = jnp.concatenate([grad_q, grad_k.reshape(row_count, local_width), grad_v], 1)
    grad_wqkv = jnp.dot(normed_low.T, grad_joined, preferred_element_type=jnp.float32).reshape(
        D, 3, local_width
    )
    back_one_partial = jnp.dot(grad_joined, qkv_matrix.T, preferred_element_type=jnp.float32)
    grad_normed = lax.psum(back_one_partial.astype(jnp.bfloat16), "tensor").astype(jnp.float32)
    input_grad = (
        grad_middle + normalize_back(grad_normed, unit_one, inverse_one, params[0])
    ).astype(jnp.bfloat16)

    def place_slice(share, total):
        return lax.dynamic_update_slice_in_dim(
            jnp.zeros((total,), jnp.float32), share, tensor_rank * share.shape[0], 0
        )

    first_rows = jnp.stack(
        [
            head_only * jnp.sum(grad_normed * unit_one, 0),
            head_only * jnp.sum(grad_normed, 0),
            place_slice(jnp.sum(grad_q.astype(jnp.float32), 0), D),
            place_slice(jnp.sum(grad_v.astype(jnp.float32), 0), D),
            head_only * jnp.sum(grad_middle, 0),
            head_only * jnp.sum(grad_normed_two * unit_two, 0),
            head_only * jnp.sum(grad_normed_two, 0),
            head_only * jnp.sum(grad_output, 0),
        ]
    )
    vector_grad = jnp.concatenate(
        [first_rows, place_slice(jnp.sum(grad_pre.astype(jnp.float32), 0), FF).reshape(FF // D, D)],
        0,
    )
    reduced_qkv, reduced_out, reduced_fc, reduced_proj, reduced_vec = (
        lax.psum_scatter(
            grad_wqkv.astype(jnp.bfloat16), "dp", scatter_dimension=0, tiled=True
        ).astype(jnp.float32),
        lax.psum_scatter(
            grad_wout.astype(jnp.bfloat16), "dp", scatter_dimension=1, tiled=True
        ).astype(jnp.float32),
        lax.psum_scatter(
            grad_fc.astype(jnp.bfloat16), "dp", scatter_dimension=0, tiled=True
        ).astype(jnp.float32),
        lax.psum_scatter(
            grad_proj.astype(jnp.bfloat16), "dp", scatter_dimension=1, tiled=True
        ).astype(jnp.float32),
        lax.psum_scatter(
            vector_grad.astype(jnp.bfloat16), "dp", scatter_dimension=1, tiled=True
        ).astype(jnp.float32),
    )
    matrix_squares = (
        jnp.sum(reduced_qkv * reduced_qkv)
        + jnp.sum(reduced_out * reduced_out)
        + jnp.sum(reduced_fc * reduced_fc)
        + jnp.sum(reduced_proj * reduced_proj)
    )
    reduced_vec = lax.psum(reduced_vec, "tensor")
    squares = lax.psum(
        matrix_squares + head_only * jnp.sum(reduced_vec * reduced_vec), ("dp", "tensor")
    )
    global_norm = jnp.sqrt(squares)
    clip_factor = max_norm / jnp.maximum(global_norm, max_norm)
    new_qkv, mean_qkv, square_qkv = adam_step(
        w_qkv, reduced_qkv * clip_factor, first_qkv, second_qkv, rate_qkv, decay_rate
    )
    new_out, mean_out, square_out = adam_step(
        w_out, reduced_out * clip_factor, first_out, second_out, rate_out, decay_rate
    )
    new_fc, mean_fc, square_fc = adam_step(
        w_fc, reduced_fc * clip_factor, first_fc, second_fc, rate_fc, decay_rate
    )
    new_proj, mean_proj, square_proj = adam_step(
        w_proj, reduced_proj * clip_factor, first_proj, second_proj, rate_proj, decay_rate
    )
    new_vec, mean_vec, square_vec = adam_step(
        vectors, reduced_vec * clip_factor, first_vec, second_vec, rate_vec, 0.0
    )
    return (
        output,
        input_grad,
        global_norm,
        new_qkv,
        new_out,
        new_fc,
        new_proj,
        new_vec,
        mean_qkv,
        mean_out,
        mean_fc,
        mean_proj,
        mean_vec,
        square_qkv,
        square_out,
        square_fc,
        square_proj,
        square_vec,
    )


def solution(mesh):
    in_specs = (
        P("dp", None),
        P("dp", None),
        P("dp", None),
        P("dp", None, "tensor"),
        P("tensor", "dp"),
        P("dp", "tensor"),
        P("tensor", "dp"),
        P(None, "dp"),
        P("dp", None, "tensor"),
        P("tensor", "dp"),
        P("dp", "tensor"),
        P("tensor", "dp"),
        P(None, "dp"),
        P("dp", None, "tensor"),
        P("tensor", "dp"),
        P("dp", "tensor"),
        P("tensor", "dp"),
        P(None, "dp"),
    )
    out_specs = (
        P("dp", None),
        P("dp", None),
        P(),
        P("dp", None, "tensor"),
        P("tensor", "dp"),
        P("dp", "tensor"),
        P("tensor", "dp"),
        P(None, "dp"),
        P("dp", None, "tensor"),
        P("tensor", "dp"),
        P("dp", "tensor"),
        P("tensor", "dp"),
        P(None, "dp"),
        P("dp", None, "tensor"),
        P("tensor", "dp"),
        P("dp", "tensor"),
        P("tensor", "dp"),
        P(None, "dp"),
    )
    return jax.shard_map(body, mesh=mesh, in_specs=in_specs, out_specs=out_specs, check_vma=False)
```

profile of v0, /device:TPU:0, one launch (start us, length us, event | category | flops | bytes accessed | tf_op | source)
XLA Modules:
  0.0 911.8 jit_solution(17150436964601841083)
XLA Ops:
  15.7 32.2 %all-gather = bf16[8,96,12]{1,2,0:T(8,128)(2,1)S(1)} all-gather(bf16[1,96,12]{1,2,0:T(8,128)(2,1)S(1)} %convert_bitcast_fusion), channel_id=1, replica_groups=mesh['dp'=8,'tensor'=4] {'dp'}, dimensions={0}, use_global_device_ids=true | all-gather | bytes 20736 | tf_op jit(solution)/shard_map/all_gather | solution.py:129
  49.0 33.4 %all_gather.17 = bf16[192,768]{0,1:T(8,128)(2,1)} all-gather(bf16[192,96]{0,1:T(8,128)(2,1)S(1)} %copy.97), channel_id=1, replica_groups=mesh['dp'=8,'tensor'=4] {'dp'}, dimensions={1}, use_global_device_ids=true | all-gather | bytes 331776 | tf_op jit(solution)/shard_map/all_gather | solution.py:126
  82.4 38.2 %all_gather.16 = bf16[768,3,192]{2,1,0:T(4,128)(2,1)S(1)} all-gather(bf16[96,3,192]{2,1,0:T(4,128)(2,1)S(1)} %copy.91), channel_id=1, replica_groups=mesh['dp'=8,'tensor'=4] {'dp'}, dimensions={0}, use_global_device_ids=true | all-gather | bytes 995328 | tf_op jit(solution)/shard_map/all_gather | solution.py:125
  148.1 45.4 %while.26 = (s32[]{:T(128)}, bf16[3,1024,3,64]{1,3,2,0:T(8,128)(2,1)}, f32[3,3,1024]{2,1,0:T(4,128)}, bf16[3,1024,3,64]{1,3,2,0:T(8,128)(2,1)}, s32[3,1024]{1,0:...) while((s32[]{:T(128)}, ...), condition=%wide.region_5.6_spmd, body=%wide.region_2.5_spmd.sunk | while | flops 846197760 | bytes 48220288 | solution.py:154
  203.5 91.4 %all-reduce.5.cloned.1.call-done = bf16[3072,768]{1,0:T(8,128)(2,1)} async-done(((bf16[3072,768]{1,0:T(8,128)(2,1)}), bf16[3072,768]{1,0:T(8,128)(2,1)}) %all-reduce.5.cloned.1.call-update) | async-done | bytes 4718608 | tf_op jit(solution)/shard_map/psum | solution.py:159
  308.7 10.1 %fusion.134 = f32[3072,768]{1,0:T(8,128)} fusion(bf16[3072,768]{1,0:T(8,128)(2,1)} %add_convert_fusion.1, bf16[768,768]{1,0:T(8,128)(2,1)} %all-gather.4.cloned.1.call-done), kind=kOutput, calls=%fused_computation.210 | convolution fusion | flops 3623878656 | bytes 15335424 | tf_op jit(solution)/shard_map/dot_general | solution.py:164
  318.8 14.0 %convert_reduce_fusion.4 = (bf16[768]{0:T(1024)(128)(2,1)}, bf16[3072,768]{1,0:T(8,128)(2,1)S(1)}) fusion(f32[3072,768]{1,0:T(8,128)} %fusion.134, f32[768]{0:T(1024)S(1)} %dynamic_slice.44, bf16[3072,768]{1,0:T(8,128)(2,1)} %param.23, bf16[768,768]{0,1:T(8,128)(2,1)} %all-gather.6.cloned.1.call-done), kind=kOutput, calls=%fused_computation.116 | convolution fusion | flops 3682860288 | bytes 20058624 | tf_op jit(solution)/shard_map/dot_general | solution.py:174
  341.1 11.0 %convolution_convert_fusion.6 = bf16[768,768]{0,1:T(8,128)(2,1)} fusion(bf16[3072,768]{1,0:T(8,128)(2,1)} %param.23, f32[3072,768]{1,0:T(8,128)} %fusion.134, f32[768]{0:T(1024)S(1)} %dynamic_slice.44), kind=kOutput, calls=%fused_computation.139 | convolution fusion | flops 3648061440 | bytes 15338496 | tf_op jit(solution)/shard_map/dot_general | solution.py:173
  352.2 8.8 convolution_convert_fusion.7
  361.1 74.3 %all-reduce.7.cloned.1.call-done = bf16[3072,768]{1,0:T(8,128)(2,1)} async-done(((bf16[3072,768]{1,0:T(8,128)(2,1)}), bf16[3072,768]{1,0:T(8,128)(2,1)}) %all-reduce.7.cloned.1.call-update) | async-done | bytes 4718608 | tf_op jit(solution)/shard_map/psum | solution.py:180
  435.4 9.5 %fusion.92 = (f32[768]{0:T(1024)}, f32[3072]{0:T(1024)S(1)}, f32[3072]{0:T(1024)S(1)}, f32[768]{0:T(1024)}) fusion(bf16[3072,768]{1,0:T(8,128)(2,1)} %all-reduce.7.cloned.1.call-done, f32[3072]{0:T(1024)S(1)} %add_rsqrt_fusion, f32[3072]{0:T(1024)S(1)} %broadcast_multiply_fusion.4, f32[768]{0:T(1024)S(1)} %copy-done.35, ...), kind=kLoop, calls=%fused_computation.114 | loop fusion | flops 33022464 | bytes 14217216 | tf_op jit(solution)/shard_map/reduce_sum | solution.py:215
  444.9 9.7 %fusion.132 = (f32[768]{0:T(1024)}, f32[3072,768]{1,0:T(8,128)S(1)}, f32[768]{0:T(1024)}) fusion(f32[3072]{0:T(1024)S(1)} %broadcast_multiply_fusion.2, f32[3072]{0:T(1024)S(1)} %broadcast_multiply_fusion.4, f32[768]{0:T(1024)S(1)} %copy-done.35, bf16[3072,768]{1,0:T(8,128)(2,1)} %all-reduce.5.cloned.1.call-done, bf16[3072,768]{1,0:T(8,128)(2,1)} %param.22, ...), kind=kLoop, calls=%fused_computation.208 | loop fusion | flops 37747200 | bytes 28372992 | tf_op jit(solution)/shard_map/reduce_sum | solution.py:214
  465.9 83.3 %while.27 = (s32[]{:T(128)}, bf16[3,1024,3,64]{1,3,2,0:T(8,128)(2,1)}, bf16[3,1024,3,64]{1,3,2,0:T(8,128)(2,1)}, bf16[3,1024,3,64]{1,3,2,0:T(8,128)(2,1)}, bf16[...) while((s32[]{:T(128)}, ...), condition=%wide.region_15.16_spmd, body=%wide.region_13.15_spmd.sunk | while | flops 2064577536 | bytes 107328664 | solution.py:187
  473.7 8.2 multiply_reduce_fusion.4
  481.9 7.0 multiply_convert_fusion.11
  501.4 8.2 multiply_reduce_fusion.4
  529.0 8.2 multiply_reduce_fusion.4
  575.7 12.4 %convolution_convert_fusion.2 = bf16[3072,768]{1,0:T(8,128)(2,1)} fusion(bf16[768,768]{0,1:T(8,128)(2,1)} %all-gather.6.cloned.1.call-done, f32[3072,768]{1,0:T(8,128)} %fusion.134, f32[768]{0:T(1024)S(1)} %copy-done.59), kind=kOutput, calls=%fused_computation.124 | convolution fusion | flops 3649830912 | bytes 15338496 | tf_op jit(solution)/shard_map/dot_general | solution.py:167
  598.8 26.7 %reduce-scatter.16.cloned.1.call-done = bf16[96,192]{1,0:T(8,128)(2,1)} async-done(((bf16[768,192]{1,0:T(8,128)(2,1)}), bf16[96,192]{1,0:T(8,128)(2,1)}) %reduce-scatter.16.cloned.1.call-update) | async-done | bytes 36880
  627.1 64.9 %reduce-scatter.10.cloned.1.call-done = bf16[96,3,192]{2,0,1:T(8,128)(2,1)} async-done(((bf16[768,3,192]{2,0,1:T(8,128)(2,1)}), bf16[96,3,192]{2,0,1:T(8,128)(2,1)}) %reduce-scatter.10.cloned.1.call-update) | async-done | bytes 110608 | tf_op jit(solution)/shard_map/reduce_scatter | solution.py:225
  696.2 67.9 %all-reduce.9.cloned.1.call-done = (bf16[3072,768]{1,0:T(8,128)(2,1)}, bf16[3072,768]{1,0:T(8,128)(2,1)}) async-done(((bf16[3072,768]{1,0:T(8,128)(2,1)}, bf16[3072,768]{1,0:T(8,128)(2,1)}), (bf16[3072,768]{1,0:T(8,128)(2,1)}, bf16[3072,768]{1,0:T(8,128)(2,1)})) %all-reduce.9.cloned.1.call-update) | async-done | bytes 9437200 | tf_op jit(solution)/shard_map/psum | solution.py:170
  772.1 61.5 %reduce-scatter.18.cloned.1.call-done = bf16[96,12]{1,0:T(8,128)(2,1)} async-done(((bf16[768,12]{1,0:T(8,128)(2,1)}), bf16[96,12]{1,0:T(8,128)(2,1)}) %reduce-scatter.18.cloned.1.call-update) | async-done | bytes 2320
  841.8 15.9 %fusion.75 = (bf16[3072,768]{1,0:T(8,128)(2,1)}, bf16[3072,768]{1,0:T(8,128)(2,1)}) fusion(f32[3072,768]{1,0:T(8,128)} %copy-done.1, bf16[3072,768]{1,0:T(8,128)(2,1)} %param.22, bf16[3072,768]{1,0:T(8,128)(2,1)} %get-tuple-element.232, f32[3072]{0:T(1024)S(1)} %broadcast_multiply_fusion, f32[3072]{0:T(1024)S(1)} %broadcast_multiply_fusion.1, ...), kind=kLoop, calls=%fused_computation.97 | loop fusion | flops 42467328 | bytes 37807104 | tf_op jit(solution)/shard_map/convert_element_type | solution.py:201
  857.7 40.2 %psum.47 = f32[]{:T(128)} all-reduce(f32[]{:T(128)S(6)} %add.276), channel_id=1, replica_groups=mesh['dp'=8,'tensor'=4] {'dp','tensor'}, use_global_device_ids=true, to_apply=%region_39.40 | all-reduce | flops 1 | bytes 8 | tf_op jit(solution)/shard_map/psum | solution.py:248
  (305 shorter events, 235.9 us)
Async XLA Ops:
  8.0 286.9 %all-reduce.5.cloned.1.call-start = ((), (), s32[]{:S(2)}) async-start(), calls=%async_computation.5 | async-start | bytes 9437184 | tf_op jit(solution)/shard_map/psum | solution.py:159
  11.9 109.6 %copy-start.37 = (f32[3072]{0:T(1024)}, f32[3072]{0:T(1024)S(1)}, u32[]{:S(2)}) copy-start(f32[3072]{0:T(1024)S(1)} %broadcast_multiply_fusion.5) | copy-start | bytes 36868
  15.7 105.7 %copy-start.40 = (f32[3072]{0:T(1024)}, f32[3072]{0:T(1024)S(1)}, u32[]{:S(2)}) copy-start(f32[3072]{0:T(1024)S(1)} %add_rsqrt_fusion.1) | copy-start | bytes 36868
  48.7 72.8 %copy-start.46 = (f32[768]{0:T(1024)}, f32[768]{0:T(1024)S(1)}, u32[]{:S(2)}) copy-start(f32[768]{0:T(1024)S(1)} %get-tuple-element.261) | copy-start | bytes 9220
  48.7 72.8 %copy-start.57 = (f32[768]{0:T(1024)}, f32[768]{0:T(1024)S(1)}, u32[]{:S(2)}) copy-start(f32[768]{0:T(1024)S(1)} %get-tuple-element.262) | copy-start | bytes 9220
  195.8 99.1 %copy-start.35 = (f32[768]{0:T(1024)S(1)}, f32[768]{0:T(1024)}, u32[]{:S(2)}) copy-start(f32[768]{0:T(1024)} %get-tuple-element.263) | copy-start | bytes 9220
  201.1 99.4 %slice-start = ((s8[4718592]{0:T(1024)(128)(4,1)}), s8[524288]{0:T(1024)(128)(4,1)S(1)}, s32[]{:S(2)}) async-start(s8[4718592]{0:T(1024)(128)(4,1)} %bitcast.168), calls=%async_computation.15 | async-start | bytes 1048576
  201.1 107.6 %all-gather.4.cloned.1.call-start = ((), (), s32[]{:S(2)}) async-start(), calls=%async_computation.6 | async-start | bytes 1327104 | tf_op jit(solution)/shard_map/all_gather | solution.py:127
  201.9 117.0 %all-gather.6.cloned.1.call-start = ((), (), s32[]{:S(2)}) async-start(), calls=%async_computation.7 | async-start | bytes 1327104 | tf_op jit(solution)/shard_map/all_gather | solution.py:128
  202.6 232.8 %all-reduce.7.cloned.1.call-start = ((), (), s32[]{:S(2)}) async-start(), calls=%async_computation.8 | async-start | bytes 9437184 | tf_op jit(solution)/shard_map/psum | solution.py:180
  203.5 137.6 %copy-start.58 = (f32[768]{0:T(1024)}, f32[768]{0:T(1024)S(1)}, u32[]{:S(2)}) copy-start(f32[768]{0:T(1024)S(1)} %dynamic_slice.44) | copy-start | bytes 9220
  341.0 254.6 %reduce-scatter.14.cloned.1.call-start = ((), (), s32[]{:S(2)}) async-start(), calls=%async_computation.11 | async-start | bytes 1327104 | tf_op jit(solution)/shard_map/reduce_scatter | solution.py:234
  352.1 245.1 %reduce-scatter.12.cloned.1.call-start = ((), (), s32[]{:S(2)}) async-start(), calls=%async_computation.10 | async-start | bytes 1327104 | tf_op jit(solution)/shard_map/reduce_scatter | solution.py:231
  361.0 264.5 %reduce-scatter.16.cloned.1.call-start = ((), (), s32[]{:S(2)}) async-start(), calls=%async_computation.12 | async-start | bytes 442368
  465.9 83.4 %copy-start.7 = (bf16[24,8,3,1024]{3,1,2,0:T(8,128)(2,1)S(1)}, bf16[24,8,3,1024]{3,1,2,0:T(8,128)(2,1)}, u32[]{:S(2)}) copy-start(bf16[24,8,3,1024]{3,1,2,0:T(8,128)(2,1)} %copy-done.6) | copy-start | bytes 3538948
  563.8 128.2 %reduce-scatter.10.cloned.1.call-start = ((), (), s32[]{:S(2)}) async-start(), calls=%async_computation.9 | async-start | bytes 1327104 | tf_op jit(solution)/shard_map/reduce_scatter | solution.py:225
  575.4 188.7 %all-reduce.9.cloned.1.call-start = ((), (), s32[]{:S(2)}) async-start(), calls=%async_computation.14 | async-start | bytes 18874368 | tf_op jit(solution)/shard_map/psum | solution.py:170
  593.6 170.5 %copy-start.41 = (f32[3072]{0:T(1024)S(1)}, f32[3072]{0:T(1024)}, u32[]{:S(2)}) copy-start(f32[3072]{0:T(1024)} %copy-done.40) | copy-start | bytes 36868
  593.7 247.9 %copy-start.36 = (f32[768]{0:T(1024)S(1)}, f32[768]{0:T(1024)}, u32[]{:S(2)}) copy-start(f32[768]{0:T(1024)} %get-tuple-element.263) | copy-start | bytes 9220
  593.7 247.9 %copy-start.49 = (f32[768]{0:T(1024)S(1)}, f32[768]{0:T(1024)}, u32[]{:S(2)}) copy-start(f32[768]{0:T(1024)} %get-tuple-element.266) | copy-start | bytes 9220
  593.7 239.9 %reduce-scatter.18.cloned.1.call-start = ((), (), s32[]{:S(2)}) async-start(), calls=%async_computation.13 | async-start | bytes 221184
  841.8 60.5 %copy-start.19 = (f32[96,3,192]{2,0,1:T(8,128)S(1)}, f32[96,3,192]{2,0,1:T(8,128)}, u32[]{:S(2)}) copy-start(f32[96,3,192]{2,0,1:T(8,128)} %param.25) | copy-start | bytes 663556
  841.8 60.5 %copy-start.25 = (bf16[96,3,192]{2,0,1:T(8,128)(2,1)S(1)}, bf16[96,3,192]{2,0,1:T(8,128)(2,1)}, u32[]{:S(2)}) copy-start(bf16[96,3,192]{2,0,1:T(8,128)(2,1)} %reduce-scatter.10.cloned.1.call-done) | copy-start | bytes 331780
  841.8 60.4 %copy-start.33 = (f32[96,3,192]{2,0,1:T(8,128)S(1)}, f32[96,3,192]{2,0,1:T(8,128)}, u32[]{:S(2)}) copy-start(f32[96,3,192]{2,0,1:T(8,128)} %param.30) | copy-start | bytes 663556
  (55 other events, 1236.9 us)
Sparse Core Ops, SparseCore 0:
  201.2 93.6 all-reduce.4
  341.2 94.1 all-reduce.6
  593.8 170.2 all-reduce.8
Sparse Core Ops, SparseCore 1:
  204.3 41.0 all-gather.3
  248.0 39.9 all-gather.5
  352.2 64.2 reduce-scatter.13
  419.8 63.3 reduce-scatter.11
  563.9 61.6 reduce-scatter.15
  628.9 63.0 reduce-scatter.9
  772.2 61.3 reduce-scatter.17
where the time goes:
time: 916 us; the launch traced here: 912 us
  waiting for transfers between devices  387 us (42%)
  matrix products  178 us (19%)
  blocking collectives  150 us (16%)
  other arithmetic  117 us (13%)
  local copies, waits for them, and re-layouts  56.3 us (6%)
  between operations  21.7 us (2%)
    psum x1, waiting for transfers between devices, body(): lax.psum(attn_partial.astype(jnp.bfloat16), 'tensor').astype(jnp.float32)  91.4 us
    unnamed x12, waiting for transfers between devices  88.4 us
    psum x1, waiting for transfers between devices, body(): lax.psum(back_two_partial.astype(jnp.bfloat16), 'tensor')  74.3 us
    psum x1, waiting for transfers between devices, body(): lax.psum(mlp_partial.astype(jnp.bfloat16), 'tensor').astype(jnp.float32)  67.9 us
    reduce_scatter x1, waiting for transfers between devices, body(): lax.psum_scatter(grad_wqkv.astype(jnp.bfloat16), 'dp', scatter_dimension=...  64.9 us
    psum x1, blocking collectives, body(): lax.psum(matrix_squares + head_only * jnp.sum(reduced_vec * reduced_vec),...  40.2 us
    all_gather x1, blocking collectives, body(): lax.all_gather(w_qkv.astype(jnp.bfloat16), 'dp', axis=0, tiled=True)  38.2 us
    all_gather x1, blocking collectives, body(): lax.all_gather(w_out.astype(jnp.bfloat16), 'dp', axis=1, tiled=True)  33.4 us
  transfers between devices with their start and end apart: 10, of which 6 were waited for; matrix products, arithmetic and copies ran while one was open for 23% of the time, Pallas kernels for 0%

commit v1 on v0

--- a/solution.py
+++ b/solution.py
@@ -1,15 +1,20 @@
+import functools
 import math
 
 import jax
 import jax.numpy as jnp
 from jax import lax
+from jax.experimental import pallas as pl
+from jax.experimental.pallas import tpu as pltpu
 from jax.sharding import PartitionSpec as P
 
 D = 768
 HD = 64
 FF = 3072
 STEP = 10
-
+PREV = 512
+BLK = 256
+LANES = 128
 
 beta_one = 0.9
 beta_two = 0.999
@@ -21,6 +26,426 @@
 decay_rate = 0.01
 epsilon = 1e-08
 max_norm = 1.0
+
+BF = jnp.bfloat16
+F32 = jnp.float32
+VMEM_LIMIT = 62 * 2**20
+ANY = pl.BlockSpec(memory_space=pl.ANY)
+VM = pl.BlockSpec(memory_space=pltpu.VMEM)
+GELU_C = math.sqrt(2.0 / math.pi)
+
+
+def nn(a, b):
+    return lax.dot_general(a, b, (((1,), (0,)), ((), ())), preferred_element_type=F32)
+
+
+def nt(a, b):
+    return lax.dot_general(a, b, (((1,), (1,)), ((), ())), preferred_element_type=F32)
+
+
+MESH = pl.DeviceIdType.MESH
+
+
+def wait_bytes(ref, sem):
+    pltpu.make_async_copy(ref, ref, sem).wait()
+
+
+def positions():
+    d, t = lax.axis_index("dp"), lax.axis_index("tensor")
+    return d, t, lax.rem(d, 2), d // 2, t // 2, lax.rem(t, 2)
+
+
+class Gather:
+    Z, X0, Y1, Y0, X1, X1U, C, CU = range(8)
+
+    def __init__(self, n_dp, blk, vecb, w, vecg, send, recv, loc, vsend, vrecv):
+        self.n_dp, self.blk, self.vecb, self.w, self.vecg = n_dp, blk, vecb, w, vecg
+        self.send, self.recv, self.loc, self.vsend, self.vrecv = send, recv, loc, vsend, vrecv
+        self.rows = blk.shape[1]
+        self.nz = n_dp // 2
+        self.d, self.t, self.x, self.z, self.y, self.c = positions()
+        self.to_x = (self.d + 1 - 2 * self.x, self.t)
+        self.to_y = (self.d, self.t + 2 - 4 * self.y)
+        self.to_c = (self.d, self.t + 1 - 2 * self.c)
+        self.u = self.t + 2 - 4 * self.y
+        self.half = D // 2
+
+    def dp_peers(self):
+        return [(lax.rem(self.d + k, self.n_dp), self.t) for k in range(1, self.n_dp)]
+
+    def at(self, m, t, block, lanes):
+        return self.w.at[m, t, pl.ds(pl.multiple_of(block * self.rows, self.rows), self.rows), lanes]
+
+    def copy(self, m, stage, src, dst, dev):
+        pltpu.make_async_remote_copy(
+            src_ref=src, dst_ref=dst, send_sem=self.send.at[m, stage], recv_sem=self.recv.at[m, stage],
+            device_id=dev, device_id_type=MESH,
+        ).start()
+
+    def size(self, m, stage):
+        rows = (self.nz - 1) * self.rows if stage == self.Z else self.nz * self.rows
+        if stage in (self.Y0, self.C, self.CU):
+            rows = D
+        lanes = self.half if stage in (self.X0, self.Y1, self.Y0, self.X1, self.X1U) else D
+        return self.w.at[m, 0, pl.ds(0, rows), pl.ds(0, lanes)]
+
+    def got(self, m, stage):
+        wait_bytes(self.size(m, stage), self.recv.at[m, stage])
+
+    def begin(self):
+        barrier = pltpu.get_barrier_semaphore()
+        peers = self.dp_peers() + [self.to_y, self.to_c]
+        for dev in peers:
+            pl.semaphore_signal(barrier, inc=1, device_id=dev, device_id_type=MESH)
+        for m in range(3):
+            pltpu.make_async_copy(self.blk.at[m], self.at(m, self.t, self.d, pl.ds(0, D)), self.loc.at[m]).start()
+        pl.semaphore_wait(barrier, len(peers))
+        for dev in self.dp_peers():
+            pltpu.make_async_remote_copy(
+                src_ref=self.vecb, dst_ref=self.vecg.at[self.d], send_sem=self.vsend, recv_sem=self.vrecv,
+                device_id=dev, device_id_type=MESH,
+            ).start()
+        self.vecg[self.d] = self.vecb[...]
+        self.along_z(0)
+
+    def vectors(self):
+        wait_bytes(self.vecg.at[pl.ds(0, self.n_dp - 1)], self.vrecv)
+        width = D // self.n_dp
+        lane = lax.broadcasted_iota(jnp.int32, (LANES, D), 0)
+        col = lax.broadcasted_iota(jnp.int32, (LANES, D), 1)
+        total = jnp.zeros((16, D), F32)
+        for p in range(self.n_dp):
+            pick = jnp.where((col == lane + p * width) & (lane < width), 1.0, 0.0).astype(BF)
+            total += nn(self.vecg[p], pick)
+        return total
+
+    def along_z(self, m):
+        for k in range(1, self.nz):
+            dev = (lax.rem(self.d + 2 * k, self.n_dp), self.t)
+            self.copy(m, self.Z, self.blk.at[m], self.at(m, self.t, self.d, pl.ds(0, D)), dev)
+
+    def columns(self, m, stage, t, lanes, dev):
+        for zz in range(self.nz):
+            ref = self.at(m, t, 2 * zz + self.x, lanes)
+            self.copy(m, stage, ref, ref, dev)
+
+    def after_z(self, m):
+        self.got(m, self.Z)
+        pltpu.make_async_copy(self.blk.at[m], self.blk.at[m], self.loc.at[m]).wait()
+        low, high = pl.ds(0, self.half), pl.ds(self.half, self.half)
+        self.columns(m, self.Y1, self.t, high, self.to_y)
+        self.columns(m, self.X0, self.t, low, self.to_x)
+        self.columns(m, self.X1, self.t, high, self.to_x)
+
+    def after_y1(self, m):
+        self.got(m, self.Y1)
+        self.columns(m, self.X1U, self.u, pl.ds(self.half, self.half), self.to_x)
+
+    def after_x0(self, m):
+        self.got(m, self.X0)
+        ref = self.w.at[m, self.t, :, pl.ds(0, self.half)]
+        self.copy(m, self.Y0, ref, ref, self.to_y)
+
+    def after_x1(self, m):
+        self.got(m, self.X1)
+        ref = self.w.at[m, self.t]
+        self.copy(m, self.C, ref, ref, self.to_c)
+
+    def after_last(self, m):
+        self.got(m, self.Y0)
+        self.got(m, self.X1U)
+        ref = self.w.at[m, self.u]
+        self.copy(m, self.CU, ref, ref, self.to_c)
+
+    def complete(self, m):
+        self.got(m, self.C)
+        self.got(m, self.CU)
+
+    def finish(self):
+        for m in range(3):
+            for stage in range(8):
+                wait_bytes(self.size(m, stage), self.send.at[m, stage])
+        wait_bytes(self.vecg.at[pl.ds(0, self.n_dp - 1)], self.vsend)
+
+
+def ln_parts(x):
+    mean = jnp.mean(x, -1, keepdims=True)
+    centred = x - mean
+    inv = lax.rsqrt(jnp.mean(centred * centred, -1, keepdims=True) + 1e-05)
+    return centred * inv, inv
+
+
+def ln_back(e, u, inv):
+    return inv * (
+        e - jnp.mean(e, -1, keepdims=True) - u * jnp.mean(e * u, -1, keepdims=True)
+    )
+
+
+def group_tiles(rows, group):
+    base = (group // 2) * 384
+    low = lax.broadcasted_iota(jnp.int32, (rows.shape[0], LANES), 1) < HD
+    first = rows[:, base : base + 128]
+    second = rows[:, base + 128 : base + 256]
+    third = rows[:, base + 256 : base + 384]
+    if group % 2 == 0:
+        return first, second
+    second, third = pltpu.roll(second, HD, 1), pltpu.roll(third, HD, 1)
+    return jnp.where(low, second, third), third
+
+
+def ungroup_tiles(even, odd):
+    low = lax.broadcasted_iota(jnp.int32, even[0].shape, 1) < HD
+    pair = pltpu.roll(odd[0], HD, 1)
+    single = pltpu.roll(odd[1], HD, 1)
+    return even[0], jnp.where(low, even[1], pair), jnp.where(low, pair, single)
+
+
+def fwd_kernel(
+    n_dp, w_in, vec_in, tok_hbm, gcol, grow,
+    w_hbm, nrm_out, q_out, k_out, v_out, kT_out, ctx_out, mid_out, n2_out, act_out, slope_out, probs_out, out_out,
+    xw, nrm, wa, wf, wp, qm, kt, vt, ktT, vtT, ctxT, ctx, mb, mid, n2, acc, act, slope, pst,
+    in_sem, w_sem, out_sem, p_sem, *gather_refs,
+):
+    gather = Gather(n_dp, w_in, vec_in, w_hbm, *gather_refs) if n_dp else None
+    if gather:
+        gather.begin()
+    else:
+        w_hbm = w_in
+    rank = lax.axis_index("tensor")
+    own = xw.shape[0] - PREV
+    start = jnp.maximum(rank * own - PREV, 0)
+    cp_prev = pltpu.make_async_copy(tok_hbm.at[pl.ds(pl.multiple_of(start, 256), PREV)], xw.at[pl.ds(0, PREV)], in_sem.at[0])
+    cp_own = pltpu.make_async_copy(tok_hbm.at[pl.ds(pl.multiple_of(rank * own, 256), own)], xw.at[pl.ds(PREV, own)], in_sem.at[1])
+    cp_prev.start()
+    cp_own.start()
+    outs = []
+
+    def load(m, dst):
+        if gather:
+            gather.complete(m)
+        cps = [pltpu.make_async_copy(w_hbm.at[m, t], dst.at[t], w_sem.at[m, t]) for t in range(4)]
+        for cp in cps:
+            cp.start()
+        return cps
+
+    def put(src, dst):
+        cp = pltpu.make_async_copy(src, dst, out_sem.at[len(outs)])
+        cp.start()
+        outs.append(cp)
+
+    for i in range(3):
+        keys = gcol[pl.ds(i * BLK, 3 * BLK), :]
+        same = keys == grow[0:1, pl.ds(i * BLK, BLK)]
+        row = lax.broadcasted_iota(jnp.int32, (3 * BLK, BLK), 0)
+        col = lax.broadcasted_iota(jnp.int32, (3 * BLK, BLK), 1)
+        mb[i] = jnp.where(same & (row <= col + PREV), 0.0, -1e30).astype(F32)
+    cp_prev.wait()
+    cp_own.wait()
+    vec = gather.vectors() if gather else vec_in[...]
+
+    def ln_one(r, _):
+        rows = pl.ds(pl.multiple_of(r * 128, 128), 128)
+        u, _inv = ln_parts(xw[rows, :].astype(F32))
+        nrm[rows, :] = (u * vec[0:1] + vec[1:2]).astype(BF)
+        return 0
+
+    lax.fori_loop(0, xw.shape[0] // 128, ln_one, 0)
+    put(nrm, nrm_out)
+    if gather:
+        gather.after_z(0)
+        gather.along_z(1)
+        gather.after_y1(0)
+        gather.after_x0(0)
+        gather.after_z(1)
+        gather.along_z(2)
+        gather.after_x1(0)
+        gather.after_last(0)
+        gather.after_y1(1)
+        gather.after_x0(1)
+    loads = load(0, wa)
+    low = lax.broadcasted_iota(jnp.int32, (BLK, LANES), 1) < HD
+    for g in range(4):
+        loads[g].wait()
+        pair, single = group_tiles(vec[0:8], g)
+        bq_pair, bq_single, bv_pair, bv_single = pair[2:3], single[2:3], pair[3:4], single[3:4]
+
+        def qkv(rc, _):
+            rows = pl.ds(pl.multiple_of(rc * BLK, BLK), BLK)
+            x = nrm[rows, :]
+            one = nn(x, wa[g, :, 0:384])
+            two = nn(x, wa[g, :, 512:768])
+            k_pair = one[:, 128:256].astype(BF)
+            v_pair = (one[:, 256:384] + bv_pair).astype(BF)
+            kt[2 * g, rows, :] = k_pair
+            vt[2 * g, rows, :] = v_pair
+            ktT[2 * g, :, rows] = k_pair.T
+            vtT[2 * g, :, rows] = v_pair.T
+            qk, vo = two[:, 0:128], two[:, 128:256]
+            k_single = jnp.where(low, pltpu.roll(qk, HD, 1), 0.0).astype(BF)
+            v_single = jnp.where(low, vo + bv_single, 0.0)
+            kt[2 * g + 1, rows, :] = k_single
+            vt[2 * g + 1, rows, :] = pltpu.roll(v_single, HD, 1).astype(BF)
+            ktT[2 * g + 1, :, rows] = k_single.T
+            vtT[2 * g + 1, :, rows] = v_single.astype(BF).T
+
+            @pl.when(rc >= PREV // BLK)
+            def _():
+                orows = pl.ds(pl.multiple_of(rc * BLK - PREV, BLK), BLK)
+                q_pair = (one[:, 0:128] + bq_pair).astype(BF).astype(F32) * 0.125
+                q_single = (qk + bq_single).astype(BF).astype(F32) * 0.125
+                qm[3 * g, orows, :] = jnp.where(low, q_pair, 0.0).astype(BF)
+                qm[3 * g + 1, orows, :] = jnp.where(low, 0.0, q_pair).astype(BF)
+                qm[3 * g + 2, orows, :] = jnp.where(low, q_single, 0.0).astype(BF)
+
+            return 0
+
+        lax.fori_loop(0, nrm.shape[0] // BLK, qkv, 0)
+    put(qm, q_out)
+    put(kt, k_out)
+    put(vt, v_out)
+    put(ktT, kT_out)
+
+    def attend(h, _):
+        g, hh = h // 3, lax.rem(h, 3)
+        tile = 2 * g + hh // 2
+        src_half = pl.multiple_of(jnp.where(hh == 1, HD, 0), HD)
+        dst_half = pl.multiple_of(jnp.where(hh == 0, 0, HD), HD)
+        slot = lax.rem(h, 2)
+
+        @pl.when(h >= 2)
+        def _():
+            pltpu.make_async_copy(pst.at[slot], probs_out.at[h - 2], p_sem.at[slot]).wait()
+
+        for i in range(3):
+            keys = pl.ds(i * BLK, 3 * BLK)
+            mine = pl.ds(i * BLK, BLK)
+            s = nt(kt[tile, keys, :], qm[h, mine, :]) + mb[i]
+            p = jnp.exp(s - jnp.max(s, 0, keepdims=True))
+            pb = (p * (1.0 / jnp.sum(p, 0, keepdims=True))).astype(BF)
+            pst[slot, i] = pb
+            o = nn(vtT[tile, pl.ds(src_half, HD), keys], pb)
+            ctxT[tile, pl.ds(dst_half, HD), mine] = o.astype(BF)
+        pltpu.make_async_copy(pst.at[slot], probs_out.at[h], p_sem.at[slot]).start()
+        return 0
+
+    if gather:
+        gather.after_z(2)
+        gather.after_x1(1)
+        gather.after_last(1)
+        gather.after_y1(2)
+        gather.after_x0(2)
+    for g in range(4):
+        ctxT[2 * g + 1, 0:HD, :] = jnp.zeros((HD, own), BF)
+    lax.fori_loop(0, 12, attend, 0)
+    for t in range(8):
+        ctx[t] = ctxT[t].T
+    put(ctx, ctx_out)
+
+    def out_proj(rc, _):
+        rows = pl.ds(pl.multiple_of(rc * BLK, BLK), BLK)
+        total = xw[pl.ds(pl.multiple_of(rc * BLK + PREV, BLK), BLK), :].astype(F32) + vec[4:5]
+        for g in range(4):
+            total += nt(ctx[2 * g, rows, :], wa[g, :, 384:512])
+            total += nt(ctx[2 * g + 1, rows, :], wa[g, :, 640:768])
+        mid[rows, :] = total
+        u, _inv = ln_parts(total)
+        n2[rows, :] = (u * vec[5:6] + vec[6:7]).astype(BF)
+        acc[rows, :] = total + vec[7:8]
+        return 0
+
+    lax.fori_loop(0, own // BLK, out_proj, 0)
+    put(mid, mid_out)
+    put(n2, n2_out)
+    loads = load(1, wf)
+    if gather:
+        gather.after_x1(2)
+        gather.after_last(2)
+    loads += load(2, wp)
+    for t in range(4):
+        loads[t].wait()
+        loads[4 + t].wait()
+        bias = vec[8 + t : 9 + t]
+
+        def mlp(rc, _):
+            rows = pl.ds(pl.multiple_of(rc * BLK, BLK), BLK)
+            z = nn(n2[rows, :], wf[t]) + bias
+            th = jnp.tanh(GELU_C * (z + 0.044715 * z * z * z))
+            half = 0.5 * (1.0 + th)
+            low_act = (z * half).astype(BF)
+            act[t, rows, :] = low_act
+            slope[t, rows, :] = (
+                half + 0.5 * z * (1.0 - th * th) * (GELU_C * (1.0 + 3 * 0.044715 * z * z))
+            ).astype(BF)
+            acc[rows, :] += nt(low_act, wp[t])
+            return 0
+
+        lax.fori_loop(0, own // BLK, mlp, 0)
+        put(act.at[t], act_out.at[t])
+        put(slope.at[t], slope_out.at[t])
+    xw[0:own, :] = acc[...].astype(BF)
+    put(xw.at[pl.ds(0, own)], out_out)
+    for slot in range(2):
+        pltpu.make_async_copy(pst.at[slot], probs_out.at[0], p_sem.at[slot]).wait()
+    for cp in outs:
+        cp.wait()
+    if gather:
+        gather.finish()
+
+
+def forward(n_dp, w_in, vec, tokens, gcol, grow, own):
+    win = own + PREV
+    sds = jax.ShapeDtypeStruct
+    out_shape = [
+        sds((3, 4, D, D) if n_dp else (8, LANES), BF),
+        sds((win, D), BF), sds((12, own, LANES), BF), sds((8, win, LANES), BF), sds((8, win, LANES), BF),
+        sds((8, LANES, win), BF), sds((8, own, LANES), BF), sds((own, D), F32), sds((own, D), BF),
+        sds((4, own, D), BF), sds((4, own, D), BF), sds((12, 3, 3 * BLK, BLK), BF), sds((own, D), BF),
+    ]
+    scratch = [
+        pltpu.VMEM((win, D), BF), pltpu.VMEM((win, D), BF),
+        pltpu.VMEM((4, D, D), BF), pltpu.VMEM((4, D, D), BF), pltpu.VMEM((4, D, D), BF),
+        pltpu.VMEM((12, own, LANES), BF), pltpu.VMEM((8, win, LANES), BF), pltpu.VMEM((8, win, LANES), BF),
+        pltpu.VMEM((8, LANES, win), BF), pltpu.VMEM((8, LANES, win), BF),
+        pltpu.VMEM((8, LANES, own), BF), pltpu.VMEM((8, own, LANES), BF),
+        pltpu.VMEM((3, 3 * BLK, BLK), F32), pltpu.VMEM((own, D), F32), pltpu.VMEM((own, D), BF),
+        pltpu.VMEM((own, D), F32), pltpu.VMEM((4, own, D), BF), pltpu.VMEM((4, own, D), BF),
+        pltpu.VMEM((2, 3, 3 * BLK, BLK), BF),
+        pltpu.SemaphoreType.DMA((2,)), pltpu.SemaphoreType.DMA((3, 4)), pltpu.SemaphoreType.DMA((24,)),
+        pltpu.SemaphoreType.DMA((2,)),
+    ]
+    params = {}
+    if n_dp:
+        scratch += [
+            pltpu.VMEM((n_dp, 16, LANES), BF), pltpu.SemaphoreType.DMA((3, 8)), pltpu.SemaphoreType.DMA((3, 8)),
+            pltpu.SemaphoreType.DMA((3,)), pltpu.SemaphoreType.DMA, pltpu.SemaphoreType.DMA,
+        ]
+        params = dict(collective_id=1, has_side_effects=True)
+    return pl.pallas_call(
+        functools.partial(fwd_kernel, n_dp),
+        out_shape=out_shape,
+        in_specs=[ANY, VM, ANY, VM, VM],
+        out_specs=[ANY] * len(out_shape),
+        scratch_shapes=scratch,
+        compiler_params=pltpu.CompilerParams(vmem_limit_bytes=VMEM_LIMIT, **params),
+        name="forward",
+    )(w_in, vec, tokens, gcol, grow)
+
+
+def pack_blocks(w_qkv, w_out, w_fc, w_proj):
+    q, k, v, o = w_qkv[:, 0], w_qkv[:, 1], w_qkv[:, 2], w_out.T
+    pairs = [a[:, :128] for a in (q, k, v, o)]
+    singles = [a[:, 128:] for a in (q, k, v, o)]
+    return jnp.stack([jnp.concatenate(pairs + singles, 1), w_fc, w_proj.T]).astype(BF)
+
+
+def doc_inputs(documents, own):
+    rank = lax.axis_index("tensor")
+    rows = documents.shape[0]
+    gid = (documents + 8 * jnp.arange(rows, dtype=jnp.int32)[:, None]).reshape(-1)
+    padded = jnp.concatenate([jnp.full((PREV,), -1, jnp.int32), gid])
+    win = lax.dynamic_slice_in_dim(padded, rank * own, own + PREV)
+    mine = lax.dynamic_slice_in_dim(gid, rank * own, own)
+    return win[:, None], jnp.broadcast_to(mine[None], (8, own))
 
 
 def normalize(hidden, gain_row, bias_row):
@@ -265,6 +690,14 @@
     new_vec, mean_vec, square_vec = adam_step(
         vectors, reduced_vec * clip_factor, first_vec, second_vec, rate_vec, 0.0
     )
+    own = tokens.shape[0] // 4
+    n_dp = lax.axis_size("dp")
+    rows = D // n_dp
+    if rows % 16 == 0:
+        blk = pack_blocks(w_qkv, w_out, w_fc, w_proj)
+        vecb = jnp.pad(vectors.astype(jnp.bfloat16), ((0, 4), (0, LANES - rows)))
+        gcol, grow = doc_inputs(documents, own)
+        output = lax.all_gather(forward(n_dp, blk, vecb, tokens, gcol, grow, own)[-1], "tensor", axis=0, tiled=True)
     return (
         output,
         input_grad,

time: 916 us -> 972 us (1.061)
  Pallas kernels: 0 us -> 120 us
  waiting for transfers between devices: 387 us -> 337 us
    pallas_call x0 -> x1, Pallas kernels: none -> 120 us  [forward(): pl.pallas_call(functools.partial(fwd_kernel, n_dp), out_shape=out_shape,...]
    unnamed x12 -> x13, waiting for transfers between devices: 88.4 us -> 49.6 us
    psum x1, waiting for transfers between devices: 74.3 us -> 94.3 us  [body(): lax.psum(back_two_partial.astype(jnp.bfloat16), 'tensor')]
    psum x1, waiting for transfers between devices: 67.9 us -> 51.4 us  [body(): lax.psum(back_one_partial.astype(jnp.bfloat16), 'tensor')]
    reduce_scatter x1, waiting for transfers between devices: 64.9 us -> 50.6 us  [body(): lax.psum_scatter(grad_wqkv.astype(jnp.bfloat16), 'dp', scatter_dimension=...]
    dot_general x1 -> x0, matrix products: 12.4 us -> none  [body(): jnp.dot(activated_low, full_proj, preferred_element_type=jnp.float32)]
    unnamed x137 -> x156, local copies, waits for them, and re-layouts: 23.9 us -> 22.4 us
  transfers between devices with their start and end apart: 10 -> 11, of which waited for: 6 -> 5; matrix products, arithmetic and copies ran while one was open for 23% -> 9% of each run, Pallas kernels for 0% -> 12%
where the time goes in v1:
time: 972 us; the launch traced here: 967 us
  waiting for transfers between devices  337 us (35%)
  matrix products  169 us (17%)
  blocking collectives  150 us (15%)
  Pallas kernels  120 us (12%)
  other arithmetic  109 us (11%)
  local copies, waits for them, and re-layouts  58.7 us (6%)
  between operations  21.9 us (2%)
    pallas_call x1, Pallas kernels, forward(): pl.pallas_call(functools.partial(fwd_kernel, n_dp), out_shape=out_shape,...  120 us
    psum x1, waiting for transfers between devices, body(): lax.psum(back_two_partial.astype(jnp.bfloat16), 'tensor')  94.3 us
    psum x1, waiting for transfers between devices, body(): lax.psum(attn_partial.astype(jnp.bfloat16), 'tensor').astype(jnp.float32)  91.4 us
    psum x1, waiting for transfers between devices, body(): lax.psum(back_one_partial.astype(jnp.bfloat16), 'tensor')  51.4 us
    reduce_scatter x1, waiting for transfers between devices, body(): lax.psum_scatter(grad_wqkv.astype(jnp.bfloat16), 'dp', scatter_dimension=...  50.6 us
    unnamed x13, waiting for transfers between devices  49.6 us
    psum x1, blocking collectives, body(): lax.psum(matrix_squares + head_only * jnp.sum(reduced_vec * reduced_vec),...  40.5 us
    all_gather x1, blocking collectives, body(): lax.all_gather(w_qkv.astype(jnp.bfloat16), 'dp', axis=0, tiled=True)  37.7 us
  transfers between devices with their start and end apart: 11, of which 5 were waited for; matrix products, arithmetic and copies ran while one was open for 9% of the time, Pallas kernels for 12%

profile of v1, /device:TPU:0, one launch (start us, length us, event | category | flops | bytes accessed | tf_op | source)
XLA Modules:
  0.0 967.4 jit_solution(5907319184875903306)
XLA Ops:
  15.7 32.2 %all-gather = bf16[8,96,12]{1,2,0:T(8,128)(2,1)S(1)} all-gather(bf16[1,96,12]{1,2,0:T(8,128)(2,1)S(1)} %convert_bitcast_fusion), channel_id=1, replica_groups=mesh['dp'=8,'tensor'=4] {'dp'}, dimensions={0}, use_global_device_ids=true | all-gather | bytes 20736 | tf_op jit(solution)/shard_map/all_gather | solution.py:554
  49.4 33.5 %all_gather.21 = bf16[192,768]{0,1:T(8,128)(2,1)} all-gather(bf16[192,96]{0,1:T(8,128)(2,1)S(1)} %copy.94), channel_id=1, replica_groups=mesh['dp'=8,'tensor'=4] {'dp'}, dimensions={1}, use_global_device_ids=true | all-gather | bytes 331776 | tf_op jit(solution)/shard_map/all_gather | solution.py:551
  82.9 37.7 %all_gather.20 = bf16[768,3,192]{2,1,0:T(4,128)(2,1)S(1)} all-gather(bf16[96,3,192]{2,1,0:T(4,128)(2,1)S(1)} %copy.97), channel_id=1, replica_groups=mesh['dp'=8,'tensor'=4] {'dp'}, dimensions={0}, use_global_device_ids=true | all-gather | bytes 995328 | tf_op jit(solution)/shard_map/all_gather | solution.py:550
  148.2 45.4 %while.26 = (s32[]{:T(128)}, bf16[3,1024,3,64]{1,3,2,0:T(8,128)(2,1)}, f32[3,3,1024]{2,1,0:T(4,128)}, bf16[3,1024,3,64]{1,3,2,0:T(8,128)(2,1)}, s32[3,1024]{1,0:...) while((s32[]{:T(128)}, ...), condition=%wide.region_5.6_spmd, body=%wide.region_2.5_spmd.sunk | while | flops 846197760 | bytes 48220288 | solution.py:579
  203.6 91.4 %all-reduce.6.cloned.1.call-done = bf16[3072,768]{1,0:T(8,128)(2,1)} async-done(((bf16[3072,768]{1,0:T(8,128)(2,1)}), bf16[3072,768]{1,0:T(8,128)(2,1)}) %all-reduce.6.cloned.1.call-update) | async-done | bytes 4718608 | tf_op jit(solution)/shard_map/psum | solution.py:584
  304.8 10.5 %fusion.102 = f32[3072,768]{1,0:T(8,128)} fusion(bf16[768,768]{1,0:T(8,128)(2,1)} %all-gather.9.cloned.1.call-done, f32[768]{0:T(1024)S(1)} %copy-done.64, f32[768]{0:T(1024)S(1)} %copy-done.52, bf16[3072,768]{1,0:T(8,128)(2,1)} %all-reduce.6.cloned.1.call-done, bf16[3072,768]{1,0:T(8,128)(2,1)} %tok_hbm.1, f32[3072]{0:T(1024)S(1)} %add_rsqrt_fusion, ...), kind=kOutput, calls=%fused_computation.141 | convolution fusion | flops 3645112320 | bytes 20087808 | tf_op jit(solution)/shard_map/dot_general | solution.py:589
  315.4 14.0 %convert_reduce_fusion.4 = (bf16[768]{0:T(1024)(128)(2,1)}, bf16[3072,768]{1,0:T(8,128)(2,1)S(1)}) fusion(f32[3072,768]{1,0:T(8,128)} %fusion.102, f32[768]{0:T(1024)S(1)} %dynamic_slice.52, bf16[3072,768]{1,0:T(8,128)(2,1)} %param.23, bf16[768,768]{0,1:T(8,128)(2,1)} %all-gather.7.cloned.1.call-done), kind=kOutput, calls=%fused_computation.116 | convolution fusion | flops 3682860288 | bytes 20058624 | tf_op jit(solution)/shard_map/dot_general | solution.py:599
  337.2 94.3 %all-reduce.8.cloned.1.call-done = bf16[3072,768]{1,0:T(8,128)(2,1)} async-done(((bf16[3072,768]{1,0:T(8,128)(2,1)}), bf16[3072,768]{1,0:T(8,128)(2,1)}) %all-reduce.8.cloned.1.call-update) | async-done | bytes 4718608 | tf_op jit(solution)/shard_map/psum | solution.py:605
  431.5 9.6 fusion.92
  441.1 9.6 fusion.142
  461.1 82.5 %while.27 = (s32[]{:T(128)}, bf16[3,1024,3,64]{1,3,2,0:T(8,128)(2,1)}, bf16[3,1024,3,64]{1,3,2,0:T(8,128)(2,1)}, bf16[3,1024,3,64]{1,3,2,0:T(8,128)(2,1)}, bf16[...) while((s32[]{:T(128)}, ...), condition=%wide.region_14.15_spmd, body=%wide.region_12.14_spmd.sunk | while | flops 2064577536 | bytes 102610048 | solution.py:612
  468.7 8.1 multiply_reduce_fusion.4
  496.2 8.1 multiply_reduce_fusion.4
  523.6 8.1 multiply_reduce_fusion.4
  559.1 11.0 %fusion.101 = bf16[768,768]{0,1:T(8,128)(2,1)} fusion(bf16[3072,768]{1,0:T(8,128)(2,1)} %param.23, f32[3072,768]{1,0:T(8,128)} %fusion.102, f32[768]{0:T(1024)S(1)} %copy-done.67), kind=kOutput, calls=%fused_computation.138 | convolution fusion | flops 3648061440 | bytes 15338496 | tf_op jit(solution)/shard_map/dot_general | solution.py:598
  570.4 11.5 %convolution_convert_fusion.5 = bf16[768,768]{1,0:T(8,128)(2,1)} fusion(bf16[3072,768]{1,0:T(8,128)(2,1)} %copy-done.70, f32[768]{0:T(1024)S(1)} %copy-done.65, f32[768]{0:T(1024)S(1)} %copy-done.53, bf16[3072,768]{1,0:T(8,128)(2,1)} %all-reduce.6.cloned.1.call-done, bf16[3072,768]{1,0:T(8,128)(2,1)} %tok_hbm.1, f32[3072]{0:T(1024)S(1)} %copy-done.44, ...), kind=kOutput, calls=%fused_computation.139 | convolution fusion | flops 3645702144 | bytes 15369216 | tf_op jit(solution)/shard_map/dot_general | solution.py:603
  589.7 7.9 convolution_convert_fusion.6
  601.8 51.4 %all-reduce.10.cloned.1.call-done = bf16[3072,768]{1,0:T(8,128)(2,1)} async-done(((bf16[3072,768]{1,0:T(8,128)(2,1)}), bf16[3072,768]{1,0:T(8,128)(2,1)}) %all-reduce.10.cloned.1.call-update) | async-done | bytes 4718608 | tf_op jit(solution)/shard_map/psum | solution.py:623
  653.1 7.0 fusion.93
  663.6 120.1 %forward.1 = (bf16[3,4,768,768]{3,2,1,0:T(8,128)(2,1)}, bf16[1280,768]{1,0:T(8,128)(2,1)}, bf16[12,768,128]{2,1,0:T(8,128)(2,1)}, bf16[8,1280,128]{2,1,0:T(8,128...) custom-call(bf16[3,96,768]{2,1,0:T(8,128)(2,1)} %pad_maximum_fusion., ...), custom_call_target="tpu_custom_call" | custom-call | tf_op jit(solution)/shard_map/forward/pallas_call | solution.py:423
  788.5 50.6 %reduce-scatter.10.cloned.1.call-done = bf16[96,3,192]{2,0,1:T(8,128)(2,1)} async-done(((bf16[768,3,192]{2,0,1:T(8,128)(2,1)}), bf16[96,3,192]{2,0,1:T(8,128)(2,1)}) %reduce-scatter.10.cloned.1.call-update) | async-done | bytes 110608 | tf_op jit(solution)/shard_map/reduce_scatter | solution.py:650
  843.5 10.7 %fusion.75 = bf16[3072,768]{1,0:T(8,128)(2,1)} fusion(f32[3072,768]{1,0:T(8,128)} %copy-done, bf16[3072,768]{1,0:T(8,128)(2,1)} %tok_hbm.1, bf16[3072,768]{1,0:T(8,128)(2,1)} %all-reduce.10.cloned.1.call-done, f32[3072]{0:T(1024)S(1)} %broadcast_multiply_fusion, f32[3072]{0:T(1024)S(1)} %broadcast_multiply_fusion.1, f32[768]{0:T(1024)S(1)} %copy-done.55, ...), kind=kLoop, calls=%fused_computation.97 | loop fusion | flops 25952256 | bytes 23645184 | tf_op jit(solution)/shard_map/convert_element_type | solution.py:626
  854.2 48.9 %reduce-scatter.18.cloned.1.call-done = bf16[96,12]{1,0:T(8,128)(2,1)} async-done(((bf16[768,12]{1,0:T(8,128)(2,1)}), bf16[96,12]{1,0:T(8,128)(2,1)}) %reduce-scatter.18.cloned.1.call-update) | async-done | bytes 2320
  910.9 40.5 %psum.39 = f32[]{:T(128)} all-reduce(f32[]{:T(128)S(6)} %add.276), channel_id=1, replica_groups=mesh['dp'=8,'tensor'=4] {'dp','tensor'}, use_global_device_ids=true, to_apply=%region_38.39 | all-reduce | flops 1 | bytes 8 | tf_op jit(solution)/shard_map/psum | solution.py:673
  (342 shorter events, 228.3 us)
Async XLA Ops:
  8.0 287.0 %all-reduce.6.cloned.1.call-start = ((), (), s32[]{:S(2)}) async-start(), calls=%async_computation.6 | async-start | bytes 9437184 | tf_op jit(solution)/shard_map/psum | solution.py:584
  11.9 109.6 %copy-start.40 = (f32[3072]{0:T(1024)}, f32[3072]{0:T(1024)S(1)}, u32[]{:S(2)}) copy-start(f32[3072]{0:T(1024)S(1)} %broadcast_multiply_fusion.5) | copy-start | bytes 36868
  201.2 103.6 %all-gather.9.cloned.1.call-start = ((), (), s32[]{:S(2)}) async-start(), calls=%async_computation.8 | async-start | bytes 1327104 | tf_op jit(solution)/shard_map/all_gather | solution.py:552
  201.9 113.4 %all-gather.7.cloned.1.call-start = ((), (), s32[]{:S(2)}) async-start(), calls=%async_computation.7 | async-start | bytes 1327104 | tf_op jit(solution)/shard_map/all_gather | solution.py:553
  202.7 228.8 %all-reduce.8.cloned.1.call-start = ((), (), s32[]{:S(2)}) async-start(), calls=%async_computation.9 | async-start | bytes 9437184 | tf_op jit(solution)/shard_map/psum | solution.py:605
  203.6 111.8 %copy-start.66 = (f32[768]{0:T(1024)}, f32[768]{0:T(1024)S(1)}, u32[]{:S(2)}) copy-start(f32[768]{0:T(1024)S(1)} %dynamic_slice.52) | copy-start | bytes 9220
  301.4 139.7 %copy-start.38 = (f32[3072]{0:T(1024)}, f32[3072]{0:T(1024)S(1)}, u32[]{:S(2)}) copy-start(f32[3072]{0:T(1024)S(1)} %broadcast_multiply_fusion.4) | copy-start | bytes 36868
  304.7 136.4 %copy-start.43 = (f32[3072]{0:T(1024)}, f32[3072]{0:T(1024)S(1)}, u32[]{:S(2)}) copy-start(f32[3072]{0:T(1024)S(1)} %add_rsqrt_fusion) | copy-start | bytes 36868
  337.1 316.0 %all-reduce.10.cloned.1.call-start = ((), (), s32[]{:S(2)}) async-start(), calls=%async_computation.10 | async-start | bytes 9437184 | tf_op jit(solution)/shard_map/psum | solution.py:623
  558.9 224.9 %reduce-scatter.14.cloned.1.call-start = ((), (), s32[]{:S(2)}) async-start(), calls=%async_computation.13 | async-start | bytes 1327104 | tf_op jit(solution)/shard_map/reduce_scatter | solution.py:659
  570.1 215.2 %reduce-scatter.12.cloned.1.call-start = ((), (), s32[]{:S(2)}) async-start(), calls=%async_computation.12 | async-start | bytes 1327104 | tf_op jit(solution)/shard_map/reduce_scatter | solution.py:656
  582.0 205.0 %reduce-scatter.16.cloned.1.call-start = ((), (), s32[]{:S(2)}) async-start(), calls=%async_computation.14 | async-start | bytes 442368
  599.9 239.2 %reduce-scatter.10.cloned.1.call-start = ((), (), s32[]{:S(2)}) async-start(), calls=%async_computation.11 | async-start | bytes 1327104 | tf_op jit(solution)/shard_map/reduce_scatter | solution.py:650
  600.6 302.4 %reduce-scatter.18.cloned.1.call-start = ((), (), s32[]{:S(2)}) async-start(), calls=%async_computation.15 | async-start | bytes 221184
  661.1 249.8 %all-gather.5.cloned.1.call-start = ((), (), s32[]{:S(2)}) async-start(), calls=%async_computation.5 | async-start | bytes 5898240 | tf_op jit(solution)/shard_map/all_gather | solution.py:700
  843.4 110.2 %copy-start.23 = (bf16[768,96]{0,1:T(8,128)(2,1)S(1)}, bf16[768,96]{0,1:T(8,128)(2,1)}, u32[]{:S(2)}) copy-start(bf16[768,96]{0,1:T(8,128)(2,1)} %reduce-scatter.14.cloned.1.call-done) | copy-start | bytes 442372
  843.4 110.2 %copy-start.31 = (f32[768,96]{0,1:T(8,128)S(1)}, f32[768,96]{0,1:T(8,128)}, u32[]{:S(2)}) copy-start(f32[768,96]{0,1:T(8,128)} %param.33) | copy-start | bytes 884740
  843.4 110.2 %copy-start.32 = (f32[768,96]{0,1:T(8,128)S(1)}, f32[768,96]{0,1:T(8,128)}, u32[]{:S(2)}) copy-start(f32[768,96]{0,1:T(8,128)} %param.38) | copy-start | bytes 884740
  843.4 111.2 %copy-start.24 = (bf16[96,768]{1,0:T(8,128)(2,1)S(1)}, bf16[96,768]{1,0:T(8,128)(2,1)}, u32[]{:S(2)}) copy-start(bf16[96,768]{1,0:T(8,128)(2,1)} %reduce-scatter.12.cloned.1.call-done) | copy-start | bytes 442372
  843.4 111.2 %copy-start.33 = (f32[96,768]{1,0:T(8,128)S(1)}, f32[96,768]{1,0:T(8,128)}, u32[]{:S(2)}) copy-start(f32[96,768]{1,0:T(8,128)} %param.32) | copy-start | bytes 884740
  843.4 111.2 %copy-start.34 = (f32[96,768]{1,0:T(8,128)S(1)}, f32[96,768]{1,0:T(8,128)}, u32[]{:S(2)}) copy-start(f32[96,768]{1,0:T(8,128)} %param.37) | copy-start | bytes 884740
  843.5 112.3 %copy-start.25 = (bf16[96,3,192]{2,0,1:T(8,128)(2,1)S(1)}, bf16[96,3,192]{2,0,1:T(8,128)(2,1)}, u32[]{:S(2)}) copy-start(bf16[96,3,192]{2,0,1:T(8,128)(2,1)} %reduce-scatter.10.cloned.1.call-done) | copy-start | bytes 331780
  843.5 112.2 %copy-start.35 = (f32[96,3,192]{2,0,1:T(8,128)S(1)}, f32[96,3,192]{2,0,1:T(8,128)}, u32[]{:S(2)}) copy-start(f32[96,3,192]{2,0,1:T(8,128)} %param.30) | copy-start | bytes 663556
  843.5 112.2 %copy-start.36 = (f32[96,3,192]{2,0,1:T(8,128)S(1)}, f32[96,3,192]{2,0,1:T(8,128)}, u32[]{:S(2)}) copy-start(f32[96,3,192]{2,0,1:T(8,128)} %param.35) | copy-start | bytes 663556
  (62 other events, 1585.6 us)
Sparse Core Ops, SparseCore 0:
  201.3 93.6 all-reduce.5
  337.2 94.1 all-reduce.7
  558.9 94.1 all-reduce.9
  783.8 46.7 all-gather.4
Sparse Core Ops, SparseCore 1:
  204.4 41.0 all-gather.8
  248.1 39.9 all-gather.6
  570.2 64.2 reduce-scatter.13
  637.9 66.3 reduce-scatter.11
  707.6 64.3 reduce-scatter.15
  775.9 63.2 reduce-scatter.9
  842.8 60.2 reduce-scatter.17
